TPU v7x, 128 devices: a whole 4x4x4 slice. The times are simulated.
128 devices in a mesh: tp: 8 (over x_hi, y), fsdp: 16 (over z, x_lo, core).
Axes of the slice: x: 4 (x_hi: 2, x_lo: 2; x = x_hi * 2 + x_lo), y: 4, z: 4, core: 2. Of those that a mesh axis runs over, the one named last changes fastest.
Arguments:
- attn_out: bfloat16 [2048, 16384], P('fsdp', 'tp')
- w_out: bfloat16 [16384, 16384], P('tp', 'fsdp')
- student: bfloat16 [2048, 8192], P('fsdp', 'tp')
- w_align: bfloat16 [8192, 16384], P('tp', 'fsdp')
- perm: int32 [2048], replicated, may hold values from 0 to 2047, as said below
Outputs:
- loss: float32 [], replicated
- grad_align: float32 [8192, 16384], P('tp', 'fsdp')
Inputs may be any that keep to these rules, and one draw needn't show every extreme that they name: `perm`: each of the 2048 teacher tokens is named by exactly one student row.
All inputs are finite; a program needn't handle non-finite values.
Results may differ from a plain program's by a relative error of at most 0.0049.
Values may be sent and summed in bfloat16 or wider, within the bound.
A program may use at most 128 MiB of HBM per device.

v0:
```python
import jax
import jax.numpy as jnp
from jax import lax
from jax.sharding import PartitionSpec as P

H = 16384


def local(attn_out, w_out, student, w_align, perm):
    attn_rows, student_rows = (
        lax.all_gather(attn_out, "fsdp", axis=0, tiled=True),
        lax.all_gather(student, "fsdp", axis=0, tiled=True),
    )
    total_rows = attn_rows.shape[0]
    block = total_rows // lax.axis_size("tp")
    first = lax.axis_index("tp") * block
    chosen = attn_rows
    teacher = lax.psum_scatter(
        jnp.dot(chosen, w_out, preferred_element_type=jnp.float32),
        "tp",
        scatter_dimension=0,
        tiled=True,
    ).astype(jnp.bfloat16)
    teacher_all = lax.all_gather(teacher, "tp", axis=0, tiled=True)
    my_perm = lax.dynamic_slice_in_dim(perm, first, block, 0)
    target = jnp.take(teacher_all, my_perm, axis=0)
    chosen = student_rows
    pred = lax.psum_scatter(
        jnp.dot(chosen, w_align, preferred_element_type=jnp.float32),
        "tp",
        scatter_dimension=0,
        tiled=True,
    )
    target32 = target.astype(jnp.float32)
    dots, sq_pred, sq_target = lax.psum(
        (
            jnp.sum(pred * target32, axis=1),
            jnp.sum(pred * pred, axis=1),
            jnp.sum(target32 * target32, axis=1),
        ),
        "fsdp",
    )
    norm_pred = jnp.sqrt(sq_pred + 1e-06)
    norm_target = jnp.sqrt(sq_target + 1e-06)
    cosine = dots / (norm_pred * norm_target)
    loss = lax.psum(jnp.sum(1.0 - cosine), "tp") / total_rows
    scale = H / 32.0
    grad_pred = (
        -scale
        * (
            target32 / (norm_pred * norm_target)[:, None]
            - (cosine / (norm_pred * norm_pred))[:, None] * pred
        )
    ).astype(jnp.bfloat16)
    grad_align = lax.dot_general(
        student_rows,
        lax.all_gather(grad_pred, "tp", axis=0, tiled=True),
        (((0,), (0,)), ((), ())),
        preferred_element_type=jnp.float32,
    )
    return (loss, grad_align)


def solution(mesh):
    placed = (P("fsdp", "tp"), P("tp", "fsdp"), P("fsdp", "tp"), P("tp", "fsdp"), P())
    return jax.shard_map(
        local, mesh=mesh, in_specs=placed, out_specs=(P(), P("tp", "fsdp")), check_vma=False
    )
```

profile of v0, /device:TPU:1, one launch (start us, length us, event | category | flops | bytes accessed | tf_op | source)
XLA Modules:
  0.0 546.7 jit_solution(89714550291330237)
XLA Ops:
  7.2 0.7 all-gather.7.cloned.1.call-update
  7.9 0.0 reduce-scatter.5.cloned.1.call-start
  8.0 57.6 %all-gather.7.cloned.1.call-done = bf16[2048,2048]{1,0:T(8,128)(2,1)} async-done(((bf16[128,2048]{1,0:T(8,128)(2,1)}), bf16[2048,2048]{1,0:T(8,128)(2,1)}) %all-gather.7.cloned.1.call-update) | async-done | bytes 8388624 | tf_op jit(solution)/shard_map/all_gather | solution.py:11
  65.5 14.4 %fusion.6 = f32[2048,1024]{1,0:T(8,128)} fusion(bf16[2048,2048]{1,0:T(8,128)(2,1)} %all-gather.7.cloned.1.call-done, bf16[2048,1024]{1,0:T(8,128)(2,1)} %param.6), kind=kOutput, calls=%fused_computation.20 | convolution fusion | flops 8589934592 | bytes 20971520 | tf_op jit(solution)/shard_map/dot_general | solution.py:19
  80.0 0.0 all-gather.5.cloned.1.call-start
  80.0 0.7 all-gather.5.cloned.1.call-update
  80.8 113.8 %reduce-scatter.5.cloned.1.call-done = f32[256,1024]{1,0:T(8,128)} async-done(((f32[2048,1024]{1,0:T(8,128)}), f32[256,1024]{1,0:T(8,128)}) %reduce-scatter.5.cloned.1.call-update) | async-done | bytes 1048592 | tf_op jit(solution)/shard_map/reduce_scatter | solution.py:18
  194.6 2.1 convert_element_type.9
  196.7 0.0 reduce-scatter.3.cloned.1.call-start
  196.8 36.0 %all-gather.5.cloned.1.call-done = bf16[2048,1024]{1,0:T(8,128)(2,1)} async-done(((bf16[128,1024]{1,0:T(8,128)(2,1)}), bf16[2048,1024]{1,0:T(8,128)(2,1)}) %all-gather.5.cloned.1.call-update) | async-done | bytes 4194320 | tf_op jit(solution)/shard_map/all_gather | solution.py:12
  232.8 9.0 %fusion.5 = f32[2048,1024]{1,0:T(8,128)} fusion(bf16[2048,1024]{1,0:T(8,128)(2,1)} %all-gather.5.cloned.1.call-done, bf16[1024,1024]{1,0:T(8,128)(2,1)S(1)} %copy-done), kind=kOutput, calls=%fused_computation.19 | convolution fusion | flops 4294967296 | bytes 14680064 | tf_op jit(solution)/shard_map/dot_general | solution.py:29
  241.8 0.0 all-gather.11.cloned.1.call-start
  241.9 0.8 compare_and_fusion
  242.6 63.7 %all-gather.9.cloned.1.call-done = bf16[2048,1024]{1,0:T(8,128)(2,1)} async-done(((bf16[256,1024]{1,0:T(8,128)(2,1)}), bf16[2048,1024]{1,0:T(8,128)(2,1)}) %all-gather.9.cloned.1.call-update) | async-done | bytes 4194320 | tf_op jit(solution)/shard_map/all_gather | solution.py:24
  306.4 4.3 gather_fusion
  310.7 111.9 %reduce-scatter.3.cloned.1.call-done = f32[256,1024]{1,0:T(8,128)} async-done(((f32[2048,1024]{1,0:T(8,128)}), f32[256,1024]{1,0:T(8,128)}) %reduce-scatter.3.cloned.1.call-update) | async-done | bytes 1048592 | tf_op jit(solution)/shard_map/reduce_scatter | solution.py:28
  422.5 1.6 multiply_reduce_fusion
  424.2 27.8 %all-reduce = (f32[256]{0:T(256)S(1)}, f32[256]{0:T(256)S(1)}, f32[256]{0:T(256)S(1)}) all-reduce(f32[256]{0:T(256)S(1)} %get-tuple-element.5, f32[256]{0:T(256)S(1)} %get-tuple-element.6, f32[256]{0:T(256)S(1)} %get-tuple-element.4), channel_id=1, replica_groups=mesh['tp'=8,'fsdp'=16] {'fsdp'}, use_global_device_ids=true, to_apply=%region_3.4 | all-reduce | flops 768 | bytes 6144 | tf_op jit(solution)/shard_map/psum | solution.py:35
  451.9 2.3 fusion.4
  454.3 0.6 subtract_reduce_fusion
  454.9 17.9 %psum.31 = f32[]{:T(128)} all-reduce(f32[]{:T(128)} %subtract_reduce_fusion), channel_id=1, replica_groups=mesh['tp'=8,'fsdp'=16] {'tp'}, use_global_device_ids=true, to_apply=%region_9.10 | all-reduce | flops 1 | bytes 8 | tf_op jit(solution)/shard_map/psum | solution.py:46
  473.4 49.9 %all-gather.11.cloned.1.call-done = bf16[2048,1024]{1,0:T(8,128)(2,1)} async-done(((bf16[256,1024]{1,0:T(8,128)(2,1)}), bf16[2048,1024]{1,0:T(8,128)(2,1)}) %all-gather.11.cloned.1.call-update) | async-done | bytes 4194320 | tf_op jit(solution)/shard_map/all_gather | solution.py:57
  523.3 10.0 %convolution_bitcast_fusion = f32[1024,1024]{0,1:T(8,128)} fusion(bf16[2048,1024]{1,0:T(8,128)(2,1)} %all-gather.11.cloned.1.call-done, bf16[2048,1024]{1,0:T(8,128)(2,1)} %all-gather.5.cloned.1.call-done), kind=kOutput, calls=%fused_computation.1 | convolution fusion | flops 4294967296 | bytes 12582912 | tf_op jit(solution)/shard_map/dot_general | solution.py:55
  533.3 5.3 copy.7
  (10 shorter events, 0.2 us)
Async XLA Ops:
  7.2 225.6 %copy-start = (bf16[1024,1024]{1,0:T(8,128)(2,1)S(1)}, bf16[1024,1024]{1,0:T(8,128)(2,1)}, u32[]{:S(2)}) copy-start(bf16[1024,1024]{1,0:T(8,128)(2,1)} %param.8) | copy-start | bytes 6291460
  7.2 58.4 %all-gather.7.cloned.1.call-start = ((), (), s32[]{:S(2)}) async-start(), calls=%async_computation.4 | async-start | bytes 8912896 | tf_op jit(solution)/shard_map/all_gather | solution.py:11
  7.9 186.7 %reduce-scatter.5.cloned.1.call-start = ((), (), s32[]{:S(2)}) async-start(), calls=%async_computation.5 | async-start | bytes 9437184 | tf_op jit(solution)/shard_map/reduce_scatter | solution.py:18
  80.0 152.8 %all-gather.5.cloned.1.call-start = ((), (), s32[]{:S(2)}) async-start(), calls=%async_computation.2 | async-start | bytes 4456448 | tf_op jit(solution)/shard_map/all_gather | solution.py:12
  80.7 225.7 %all-gather.9.cloned.1.call-start = ((), (), s32[]{:S(2)}) async-start(), calls=%async_computation.6 | async-start | bytes 4718592 | tf_op jit(solution)/shard_map/all_gather | solution.py:24
  196.7 225.8 %reduce-scatter.3.cloned.1.call-start = ((), (), s32[]{:S(2)}) async-start(), calls=%async_computation.3 | async-start | bytes 9437184 | tf_op jit(solution)/shard_map/reduce_scatter | solution.py:28
  241.8 281.5 %all-gather.11.cloned.1.call-start = ((), (), s32[]{:S(2)}) async-start(), calls=%async_computation.7 | async-start | bytes 4718592 | tf_op jit(solution)/shard_map/all_gather | solution.py:57
Sparse Core Ops, SparseCore 0:
  9.7 55.7 all-gather.6
  80.1 114.4 reduce-scatter.4
  196.4 36.3 all-gather.4
  235.9 70.4 all-gather.8
  310.5 111.9 reduce-scatter.2
  454.4 68.8 all-gather.10
where the time goes:
time: 547 us
  waiting for transfers between devices  434 us (79%)
  blocking collectives  45.6 us (8%)
  matrix products  33.4 us (6%)
  between operations  15.9 us (3%)
  local copies, waits for them, and re-layouts  9.63 us (2%)
  other arithmetic  7.45 us (1%)
    reduce_scatter x1, waiting for transfers between devices, local(): lax.psum_scatter(jnp.dot(chosen, w_out, preferred_element_type=jnp.float3...  114 us
    reduce_scatter x1, waiting for transfers between devices, local(): lax.psum_scatter(jnp.dot(chosen, w_align, preferred_element_type=jnp.floa...  112 us
    all_gather x1, waiting for transfers between devices, local(): teacher_all = lax.all_gather(teacher, 'tp', axis=0, tiled=True)  63.7 us
    all_gather x1, waiting for transfers between devices, local(): lax.all_gather(attn_out, 'fsdp', axis=0, tiled=True)  57.6 us
    all_gather x1, waiting for transfers between devices, local(): lax.all_gather(grad_pred, 'tp', axis=0, tiled=True)  49.9 us
    all_gather x1, waiting for transfers between devices, local(): lax.all_gather(student, 'fsdp', axis=0, tiled=True)  36 us
    psum x1, blocking collectives, local(): lax.psum((jnp.sum(pred * target32, axis=1), jnp.sum(pred * pred, axis=1),...  27.8 us
    psum x1, blocking collectives, local(): loss = lax.psum(jnp.sum(1.0 - cosine), 'tp') / total_rows  17.9 us
  transfers between devices with their start and end apart: 6, of which 6 were waited for; matrix products, arithmetic and copies ran while one was open for 3% of the time, Pallas kernels for 0%

commit v1 on v0

v1 whole, which is shorter than its diff:
```python
import functools

import jax
import jax.numpy as jnp
from jax import lax
from jax.experimental import pallas as pl
from jax.experimental.pallas import tpu as pltpu
from jax.sharding import PartitionSpec as P

MESH = pl.DeviceIdType.MESH
BF, F32 = jnp.bfloat16, jnp.float32

NC = 8
CH = 256
BL = 128
GR = 64
HF = 32
D1, D2, D3, D4, D5, D6, D7 = 1, 2, 3, 4, 5, 6, 7
LAST = 2 * NC - 1


def place():
    t, f = lax.axis_index("tp"), lax.axis_index("fsdp")
    return t // 4, t % 4, f // 4, (f // 2) % 2, f % 2, t, f


def kernel(attn_in, stu_in, wout_in, wal_in, perm_ref, loss_ref, grad_out,
           attn, stu, stup, wout, wal, part, rsend, rrecv, nsend, nrecv, xsend, xrecv, keep,
           town, pown, ssend, srecv, gall, acc, lacc, lrecv,
           sem_in, sem_as, sem_ar, sem_ss, sem_sr, sem_rs, sem_rr, sem_ns, sem_nr, sem_xs, sem_xr,
           sem_ts, sem_tr, sem_gs, sem_gr, sem_fs, sem_fr, sem_ls, sem_lr):
    xh, y, z, xl, c, t, f = place()
    total_rows = NC * CH

    def tp_dev(a, b):
        return {"tp": a * 4 + b, "fsdp": f}

    def fs_dev(a, b, d):
        return {"tp": t, "fsdp": a * 4 + b * 2 + d}

    zp, zm, z2 = (z + 1) % 4, (z + 3) % 4, (z + 2) % 4
    yp, ym = (y + 1) % 4, (y + 3) % 4
    y2 = (y + 2) % 4
    xo, ho, co = 1 - xl, 1 - xh, 1 - c
    Y_UP, Y_DN, X_HI = tp_dev(xh, yp), tp_dev(xh, ym), tp_dev(ho, y)
    Z_UP, Z_DN = fs_dev(zp, xl, c), fs_dev(zm, xl, c)
    X_LO, CORE = fs_dev(z, xo, c), fs_dev(z, xl, co)

    def remote(src, dst, ss, rs, dev):
        return pltpu.make_async_remote_copy(
            src_ref=src, dst_ref=dst, send_sem=ss, recv_sem=rs, device_id=dev, device_id_type=MESH)

    def rows(a, b, d):
        return (a * 4 + b * 2 + d) * BL

    own = rows(z, xl, c)
    loads = [
        pltpu.make_async_copy(attn_in, attn.at[pl.ds(own, BL)], sem_in.at[0]),
        pltpu.make_async_copy(wout_in, wout, sem_in.at[1]),
        pltpu.make_async_copy(stu_in, stu.at[pl.ds(own, BL)], sem_in.at[2]),
        pltpu.make_async_copy(wal_in, wal, sem_in.at[3]),
    ]
    for l in loads:
        l.start()

    barrier = pltpu.get_barrier_semaphore()
    for i in range(1, 16):
        pl.semaphore_signal(barrier, inc=1, device_id={"tp": t, "fsdp": (f + i) % 16}, device_id_type=MESH)
    for i in range(1, 8):
        pl.semaphore_signal(barrier, inc=1, device_id={"tp": (t + i) % 8, "fsdp": f}, device_id_type=MESH)
    pl.semaphore_wait(barrier, 22)

    blk = [(z, xl), (z, xo), (zm, xl), (zp, xl), (zm, xo), (zp, xo), (z2, xl), (z2, xo)]

    def a_rows(k, d=None, off=0, n=BL):
        return attn.at[pl.ds(rows(blk[k][0], blk[k][1], c if d is None else d) + off, n)]

    def s_rows(k, d=None, off=0, n=BL):
        return stu.at[pl.ds(rows(blk[k][0], blk[k][1], c if d is None else d) + off, n)]

    HB = BL // 2

    def a_own(src_ref, j, dev, peer_slot):
        return remote(attn_in, a_rows(0), sem_as.at[j], sem_ar.at[peer_slot], dev)

    def a_recv(k):
        return remote(a_rows(k), a_rows(k), sem_as.at[0], sem_ar.at[k], X_LO)

    def half_recv(ref_rows, k, h, sems, slot):
        r = ref_rows(k, None, h * HB, HB)
        return remote(r, r, sem_as.at[0], sems.at[slot], X_LO)

    def core_copies(ref_rows, k, send, ssem, rsem, slot):
        n = BL // 4
        out = []
        for i in range(4):
            r = ref_rows(k, None, i * n, n)
            out.append(remote(r, r, ssem.at[slot], rsem.at[slot], CORE))
        return out

    def core_whole(ref_rows, k, ssem, rsem, slot):
        r = ref_rows(k, co)
        return remote(r, r, ssem.at[slot], rsem.at[slot], CORE)

    sends = {}

    def go(name, copy):
        copy().start()
        sends[name] = copy

    s_src = stu_in
    go("a0", lambda: remote(attn_in, a_rows(0), sem_as.at[0], sem_ar.at[1], X_LO))
    go("a1", lambda: remote(attn_in, a_rows(0), sem_as.at[1], sem_ar.at[2], Z_UP))
    go("a2", lambda: remote(attn_in, a_rows(0), sem_as.at[2], sem_ar.at[3], Z_DN))
    loads[0].wait()

    def to_core(ref_rows, k, ssem, rsem, slot):
        for cp in core_copies(ref_rows, k, None, ssem, rsem, slot):
            cp.start()
        sends[ref_rows, k] = lambda: remote(ref_rows(k), ref_rows(k), ssem.at[slot], rsem.at[slot], CORE)

    to_core(a_rows, 0, sem_as, sem_ar, 10)
    go("s0", lambda: remote(stu_in, s_rows(0), sem_ss.at[0], sem_sr.at[0], Z_UP))
    go("s1", lambda: remote(stu_in, s_rows(0), sem_ss.at[1], sem_sr.at[1], Z_DN))
    go("s2", lambda: remote(stu_in, s_rows(0), sem_ss.at[2], sem_sr.at[4], X_LO))
    loads[2].wait()
    to_core(s_rows, 0, sem_ss, sem_sr, 8)
    loads[1].wait()
    loads[3].wait()
    acc[...] = jnp.zeros_like(acc)
    lacc[...] = jnp.zeros_like(lacc)

    def arrive_a(k):
        if k < 6:
            a_recv(k).wait_recv()
        else:
            half_recv(a_rows, k, 0, sem_ar, 6 + 2 * (k - 6)).wait_recv()
            half_recv(a_rows, k, 1, sem_ar, 7 + 2 * (k - 6)).wait_recv()
        if k == 1:
            go("a3", lambda: remote(a_rows(1), a_rows(1), sem_as.at[3], sem_ar.at[4], Z_UP))
            go("a4", lambda: remote(a_rows(1), a_rows(1), sem_as.at[4], sem_ar.at[5], Z_DN))
        if k in (2, 4):
            go(f"u{k}", lambda: remote(a_rows(k, None, 0, HB), a_rows(k, None, 0, HB),
                                       sem_as.at[5 + (k - 2) // 2], sem_ar.at[6 + (k - 2)], Z_UP))
        if k in (3, 5):
            go(f"d{k}", lambda: remote(a_rows(k, None, HB, HB), a_rows(k, None, HB, HB),
                                       sem_as.at[7 + (k - 3) // 2], sem_ar.at[7 + (k - 3)], Z_DN))
        to_core(a_rows, k, sem_as, sem_ar, 10 + k)

    def arrive_s(step):
        if step == 0:
            for k, slot, dev, off, out in ((2, 0, Z_UP, 0, 2), (3, 1, Z_DN, HB, 3)):
                remote(s_rows(k), s_rows(k), sem_ss.at[0], sem_sr.at[slot], X_LO).wait_recv()
                go(f"h{k}", lambda k=k, off=off, out=out, dev=dev: remote(
                    s_rows(k, None, off, HB), s_rows(k, None, off, HB), sem_ss.at[1 + out], sem_sr.at[out], dev))
                go(f"x{k}", lambda k=k, out=out: remote(
                    s_rows(k), s_rows(k), sem_ss.at[3 + out], sem_sr.at[3 + out], X_LO))
                to_core(s_rows, k, sem_ss, sem_sr, 8 + k)
        elif step == 1:
            half_recv(s_rows, 6, 0, sem_sr, 2).wait_recv()
            half_recv(s_rows, 6, 1, sem_sr, 3).wait_recv()
            go("x6", lambda: remote(s_rows(6), s_rows(6), sem_ss.at[7], sem_sr.at[7], X_LO))
            to_core(s_rows, 6, sem_ss, sem_sr, 8 + 6)
        else:
            for k, slot in ((1, 4), (4, 5), (5, 6), (7, 7)):
                remote(s_rows(k), s_rows(k), sem_ss.at[0], sem_sr.at[slot], X_LO).wait_recv()
                to_core(s_rows, k, sem_ss, sem_sr, 8 + k)

    def core_arrived(ref_rows, k, ssem, rsem, slot):
        core_whole(ref_rows, k, ssem, rsem, slot).wait_recv()

    def group(ref, slot, g, off, n):
        return ref[slot, pl.ds(g * GR + off, n), :]

    def relay(r, d):
        s = r % 4
        dev = Y_UP if d == 0 else Y_DN
        return remote(rsend.at[s, d], rrecv.at[r, d], sem_rs.at[s, d], sem_rr.at[r, d], dev)

    def near(r, d):
        s = r % 4
        dev = Y_UP if d == 0 else Y_DN
        return remote(nsend.at[s, d], nrecv.at[r, d], sem_ns.at[s, d], sem_nr.at[r, d], dev)

    def across(r):
        s = r % 4
        return remote(xsend.at[s], xrecv.at[r], sem_xs.at[s], sem_xr.at[r], X_HI)

    def stage0_send(r):
        s = r % 4
        rsend[s, 0] = group(part, s, y2, 0, HF).astype(BF)
        relay(r, 0).start()
        rsend[s, 1] = group(part, s, y2, HF, HF).astype(BF)
        relay(r, 1).start()

    def stage0_teacher(r, k):
        core_arrived(a_rows, k, sem_as, sem_ar, 10 + k)
        base = (blk[k][0] * 2 + blk[k][1]) * CH
        part[r % 4] = jnp.dot(attn[pl.ds(base, CH), :], wout[...], preferred_element_type=F32)

    def stage0_student(r):
        base = pl.multiple_of((r - NC) * CH, CH)
        row = lax.broadcasted_iota(jnp.int32, (CH, total_rows), 0) + base
        pick = jnp.where(row == perm_ref[...], 1.0, 0.0).astype(BF)
        mine = jnp.dot(pick, stu[...], preferred_element_type=F32).astype(BF)
        stup[pl.ds(base, CH), :] = mine
        part[r % 4] = jnp.dot(mine, wal[...], preferred_element_type=F32)

    def stage1(r):
        s = r % 4
        relay(r, 0).wait()
        nsend[s, 0, 0:HF, :] = (group(part, s, yp, 0, HF) + rrecv[r, 0].astype(F32)).astype(BF)
        nsend[s, 0, HF:GR, :] = group(part, s, yp, HF, HF).astype(BF)
        near(r, 0).start()
        relay(r, 1).wait()
        nsend[s, 1, 0:HF, :] = group(part, s, ym, 0, HF).astype(BF)
        nsend[s, 1, HF:GR, :] = (group(part, s, ym, HF, HF) + rrecv[r, 1].astype(F32)).astype(BF)
        near(r, 1).start()

    def stage2(r):
        s = r % 4
        near(r, 0).wait()
        near(r, 1).wait()

        def half(h):
            o = pl.multiple_of(h * HF, HF)
            return (group(part, s, y, o, HF) + nrecv[r, 0, pl.ds(o, HF), :].astype(F32)
                    + nrecv[r, 1, pl.ds(o, HF), :].astype(F32))

        xsend[s] = half(ho)
        across(r).start()
        keep[s] = half(xh)

    def stat_copy(k, i):
        return remote(ssend.at[k], srecv.at[k, f], sem_ts.at[k], sem_tr.at[k],
                      {"tp": t, "fsdp": (f + i) % 16})

    def lanes_of(cols):
        lane = lax.broadcasted_iota(jnp.int32, (HF, 128), 1)
        m = jnp.zeros((HF, 128), F32)
        for j, col in enumerate(cols):
            m = jnp.where(lane == j, col, m)
        m = jnp.concatenate([m, jnp.zeros((128 - HF, 128), F32)], axis=0)
        return m.T[0:8, :]

    def stage3(r):
        s = r % 4
        across(r).wait()
        full = keep[s] + xrecv[r]

        @pl.when(r < NC)
        def _():
            j = r // 2
            dz = jnp.where(r < 2, 0, jnp.where(r >= 6, 2, jnp.where(r % 2 == 0, 3, 1)))
            other = jnp.where(r < 2, r, jnp.where(r >= 6, r - 6, (r - 2) // 2))
            q = ((z + dz) % 4) * 2 + jnp.where(other == 0, xl, xo)
            town[q] = full.astype(BF)

        @pl.when(r >= NC)
        def _():
            k = r - NC
            tg = town[k].astype(F32)
            pown[k] = full
            ssend[k] = lanes_of([jnp.sum(full * tg, axis=1, keepdims=True),
                                 jnp.sum(full * full, axis=1, keepdims=True),
                                 jnp.sum(tg * tg, axis=1, keepdims=True)])
            srecv[k, f] = ssend[k]
            for i in range(1, 16):
                stat_copy(k, i).start()

    def g_rows(k, g, h):
        return gall.at[pl.ds(pl.multiple_of(k * CH + g * GR + h * HF, HF), HF)]

    def g_across(k, h):
        return remote(g_rows(k, y, h), g_rows(k, y, h), sem_xs.at[4 + k % 4], sem_xr.at[2 * NC + k], X_HI)

    def g_near(k, d, h, g):
        return remote(g_rows(k, g, h), g_rows(k, g, h), sem_gs.at[k % 4, d, h], sem_gr.at[k, d, h],
                      Y_UP if d == 0 else Y_DN)

    def g_far(k, d, g):
        return remote(g_rows(k, g, d), g_rows(k, g, d), sem_fs.at[k % 4, d], sem_fr.at[k, d],
                      Y_UP if d == 0 else Y_DN)

    def stage4(k):
        w = remote(srecv.at[k, pl.ds(0, 15)], srecv.at[k, pl.ds(0, 15)], sem_ts.at[k], sem_tr.at[k], CORE)
        w.wait_recv()
        w.wait_send()
        st = srecv[k, 0]
        for i in range(1, 16):
            st = st + srecv[k, i]
        dots, pp, qq = st[0:1, :], st[1:2, :], st[2:3, :]
        n_p, n_t = jnp.sqrt(pp + 1e-6), jnp.sqrt(qq + 1e-6)
        cosine = dots / (n_p * n_t)
        lane = lax.broadcasted_iota(jnp.int32, (1, 128), 1)
        lacc[0:1, :] += jnp.where(lane < HF, 1.0 - cosine, 0.0)
        scale = 16 * 1024 / 32.0
        ca = -scale / (n_p * n_t)
        cb = scale * (cosine / (n_p * n_p))
        both = jnp.concatenate([ca, cb, jnp.zeros((126, 128), F32)], axis=0).T
        g = both[0:HF, 0:1] * town[k].astype(F32) + both[0:HF, 1:2] * pown[k]
        gall[pl.ds(pl.multiple_of(k * CH + y * GR + xh * HF, HF), HF), :] = g.astype(BF)
        g_across(k, xh).start()
        g_near(k, 0, xh, y).start()
        g_near(k, 1, xh, y).start()

    def stage5(k):
        g_across(k, xh).wait_send()
        g_across(k, ho).wait_recv()
        g_near(k, 0, ho, y).start()
        g_near(k, 1, ho, y).start()

    def stage6(k):
        g_near(k, 0, 0, ym).wait_recv()
        g_far(k, 0, ym).start()
        g_near(k, 1, 1, yp).wait_recv()
        g_far(k, 1, yp).start()

    def stage7(k):
        g_near(k, 0, 1, ym).wait_recv()
        g_near(k, 1, 0, yp).wait_recv()
        g_far(k, 0, y2).wait_recv()
        g_far(k, 1, y2).wait_recv()
        for d in range(2):
            g_far(k, d, y).wait_send()
            for h in range(2):
                g_near(k, d, h, y).wait_send()
        base = pl.multiple_of(k * CH, CH)
        acc[...] += lax.dot_general(
            stup[pl.ds(base, CH), :], gall[pl.ds(base, CH), :], (((0,), (0,)), ((), ())),
            preferred_element_type=F32)

    def tick(i, carry):
        def when(lo, hi, cond_value):
            return pl.when(jnp.logical_and(cond_value >= lo, cond_value <= hi))

        for d, fn in ((D6, stage6), (D5, stage5), (D4, stage4)):
            @when(NC, LAST, i - d)
            def _(d=d, fn=fn):
                fn(i - d - NC)
        for d, fn in ((D3, stage3), (D2, stage2), (D1, stage1)):
            @when(0, LAST, i - d)
            def _(d=d, fn=fn):
                fn(i - d)
        for k in range(NC):
            @pl.when(i == k)
            def _(k=k):
                core_arrived(a_rows, k, sem_as, sem_ar, 10 + k)

        @pl.when(i < NC)
        def _():
            dz = jnp.where(i < 2, 0, jnp.where(i >= 6, 2, jnp.where(i % 2 == 0, 3, 1)))
            other = jnp.where(i < 2, i, jnp.where(i >= 6, i - 6, (i - 2) // 2))
            q = ((z + dz) % 4) * 2 + jnp.where(other == 0, xl, xo)
            base = pl.multiple_of(q * CH, CH)
            part[i % 4] = jnp.dot(attn[pl.ds(base, CH), :], wout[...], preferred_element_type=F32)

        @when(NC, LAST, i)
        def _():
            stage0_student(i)

        @pl.when(i <= LAST)
        def _():
            stage0_send(i)
        for k in range(1, NC):
            @pl.when(i == k - 1)
            def _(k=k):
                arrive_a(k)
        for step, at in ((0, 4), (1, 6), (2, 7)):
            @pl.when(i == at)
            def _(step=step):
                arrive_s(step)

        @pl.when(i == NC - 1)
        def _():
            for k in range(NC):
                core_arrived(s_rows, k, sem_ss, sem_sr, 8 + k)

        @when(NC, LAST, i - D7)
        def _():
            stage7(i - D7 - NC)
        return carry

    lax.fori_loop(0, LAST + D7 + 1, tick, 0)

    lrecv[t] = lacc[...]
    for i in range(1, 8):
        remote(lacc, lrecv.at[t], sem_ls.at[0], sem_lr.at[0], {"tp": (t + i) % 8, "fsdp": f}).start()
    out = pltpu.make_async_copy(acc, grad_out, sem_in.at[0])
    out.start()
    for copy in sends.values():
        copy().wait_send()
    w = remote(lrecv.at[pl.ds(0, 7)], lrecv.at[pl.ds(0, 7)], sem_ls.at[0], sem_lr.at[0], CORE)
    w.wait_recv()
    w.wait_send()
    total = lrecv[0]
    for i in range(1, 8):
        total = total + lrecv[i]
    loss_ref[0, 0] = jnp.sum(total) / total_rows
    out.wait()


def local(attn_out, w_out, student, w_align, perm):
    rows_all, width = NC * CH, w_out.shape[1]
    dma = pltpu.SemaphoreType.DMA
    loss, grad = pl.pallas_call(
        kernel,
        name="distill",
        out_shape=(jax.ShapeDtypeStruct((1, 1), F32),
                   jax.ShapeDtypeStruct((w_align.shape[0], width), F32)),
        in_specs=[pl.BlockSpec(memory_space=pl.ANY)] * 4 + [pl.BlockSpec(memory_space=pltpu.VMEM)],
        out_specs=(pl.BlockSpec(memory_space=pltpu.SMEM), pl.BlockSpec(memory_space=pl.ANY)),
        scratch_shapes=[
            pltpu.VMEM((rows_all, attn_out.shape[1]), BF),
            pltpu.VMEM((rows_all, student.shape[1]), BF),
            pltpu.VMEM((rows_all, student.shape[1]), BF),
            pltpu.VMEM(w_out.shape, BF),
            pltpu.VMEM(w_align.shape, BF),
            pltpu.VMEM((4, CH, width), F32),
            pltpu.VMEM((4, 2, HF, width), BF),
            pltpu.VMEM((2 * NC, 2, HF, width), BF),
            pltpu.VMEM((4, 2, GR, width), BF),
            pltpu.VMEM((2 * NC, 2, GR, width), BF),
            pltpu.VMEM((4, HF, width), F32),
            pltpu.VMEM((2 * NC, HF, width), F32),
            pltpu.VMEM((4, HF, width), F32),
            pltpu.VMEM((NC, HF, width), BF),
            pltpu.VMEM((NC, HF, width), F32),
            pltpu.VMEM((NC, 8, 128), F32),
            pltpu.VMEM((NC, 16, 8, 128), F32),
            pltpu.VMEM((rows_all, width), BF),
            pltpu.VMEM((w_align.shape[0], width), F32),
            pltpu.VMEM((8, 128), F32),
            pltpu.VMEM((8, 8, 128), F32),
            dma((4,)),
            dma((18,)), dma((18,)), dma((16,)), dma((16,)),
            dma((4, 2)), dma((2 * NC, 2)),
            dma((4, 2)), dma((2 * NC, 2)),
            dma((8,)), dma((3 * NC,)),
            dma((NC,)), dma((NC,)),
            dma((4, 2, 2)), dma((NC, 2, 2)),
            dma((4, 2)), dma((NC, 2)),
            dma((1,)), dma((1,)),
        ],
        compiler_params=pltpu.CompilerParams(
            collective_id=0, has_side_effects=True, vmem_limit_bytes=60 * 2**20),
    )(attn_out, student, w_out, w_align, perm.reshape(1, -1))
    return loss.reshape(()), grad


def solution(mesh):
    placed = (P("fsdp", "tp"), P("tp", "fsdp"), P("fsdp", "tp"), P("tp", "fsdp"), P())
    return jax.shard_map(
        local, mesh=mesh, in_specs=placed, out_specs=(P(), P("tp", "fsdp")), check_vma=False
    )
```

time: 547 us -> 172 us (0.31)
  waiting for transfers between devices: 434 us -> 0 us
  Pallas kernels: 0 us -> 163 us
  blocking collectives: 45.6 us -> 0 us
  matrix products: 33.4 us -> 0 us
  between operations: 15.9 us -> 2.37 us
  other arithmetic: 7.45 us -> 0 us
    reduce_scatter x2 -> x0, waiting for transfers between devices: 226 us -> none  [the longest x1 114 us: local(): lax.psum_scatter(jnp.dot(chosen, w_out, preferred_element_type=jnp.float3...]
    all_gather x4 -> x0, waiting for transfers between devices: 207 us -> none  [the longest x1 63.7 us: local(): teacher_all = lax.all_gather(teacher, 'tp', axis=0, tiled=True)]
    pallas_call x0 -> x1, Pallas kernels: none -> 163 us  [local(): pl.pallas_call(kernel, name='distill', out_shape=(jax.ShapeDtypeStruct((1...]
    psum x2 -> x0, blocking collectives: 45.6 us -> none  [the longest x1 27.8 us: local(): lax.psum((jnp.sum(pred * target32, axis=1), jnp.sum(pred * pred, axis=1),...]
    dot_general x3 -> x0, matrix products: 33.4 us -> none  [the longest x1 14.4 us: local(): jnp.dot(chosen, w_out, preferred_element_type=jnp.float32)]
  transfers between devices with their start and end apart: 6 -> 0, of which waited for: 6 -> 0; matrix products, arithmetic and copies ran while one was open for 3% -> 0% of each run, Pallas kernels for 0% -> 0%
where the time goes in v1:
time: 172 us; the launch traced here: 170 us
  Pallas kernels  163 us (95%)
  local copies, waits for them, and re-layouts  4.79 us (3%)
  between operations  2.37 us (1%)
    pallas_call x1, Pallas kernels, local(): pl.pallas_call(kernel, name='distill', out_shape=(jax.ShapeDtypeStruct((1...  163 us
    unnamed x1, local copies, waits for them, and re-layouts  4.79 us

profile of v1, /device:TPU:1, one launch (start us, length us, event | category | flops | bytes accessed | tf_op | source)
XLA Modules:
  0.0 170.2 jit_solution(2335462935974101779)
XLA Ops:
  0.6 163.0 %distill.1 = (f32[1,1]{1,0:T(1,128)}, f32[1024,1024]{1,0:T(8,128)}) custom-call(bf16[128,2048]{1,0:T(8,128)(2,1)} %attn_in.1, bf16[128,1024]{1,0:T(8,128)(2,1)} %stu_in.1, bf16[2048,1024]{1,0:T(8,128)(2,1)} %wout_in.1, bf16[1024,1024]{1,0:T(8,128)(2,1)} %wal_in.1, s32[1,2048]{1,0:T(1,128)} %bitcast.2), custom_call_target="tpu_custom_call" | custom-call | tf_op jit(solution)/shard_map/distill/pallas_call | solution.py:406
  164.2 4.8 %copy.10 = f32[1024,1024]{1,0:T(8,128)} copy(f32[1024,1024]{1,0:T(8,128)} %get-tuple-element.9) | data formatting | bytes 8388608

commit v2 on v1

v2 whole, which is shorter than its diff:
```python
import functools

import jax
import jax.numpy as jnp
from jax import lax
from jax.experimental import pallas as pl
from jax.experimental.pallas import tpu as pltpu
from jax.sharding import PartitionSpec as P

MESH = pl.DeviceIdType.MESH
BF, F32 = jnp.bfloat16, jnp.float32

NC = 8
CH = 256
BL = 128
NS = 8
HB = 64
GR = 64
HF = 32
D1, D2, D3, D4, D5, D6, D7 = 2, 4, 6, 8, 10, 12, 14
LAST = 2 * NC - 1


def place():
    t, f = lax.axis_index("tp"), lax.axis_index("fsdp")
    return t // 4, t % 4, f // 4, (f // 2) % 2, f % 2, t, f


def kernel(attn_in, stu_in, wout_in, wal_in, perm_ref, loss_ref, acc_out, stu_out, g_out,
           attn, stu, stup, wout, wal, part, rsend, rrecv, nsend, nrecv, xsend, xrecv, keep,
           town, pown, stut, ssend, srecv, gall, acc, lacc, lrecv,
           sem_in, sem_as, sem_ar, sem_cs, sem_cr, sem_ss, sem_sr, sem_rs, sem_rr, sem_ns, sem_nr, sem_xs, sem_xr,
           sem_ts, sem_tr, sem_gs, sem_gr, sem_fs, sem_fr, sem_ls, sem_lr):
    xh, y, z, xl, c, t, f = place()
    total_rows = NC * CH

    def tp_dev(a, b):
        return {"tp": a * 4 + b, "fsdp": f}

    def fs_dev(a, b, d):
        return {"tp": t, "fsdp": a * 4 + b * 2 + d}

    zp, zm, z2 = (z + 1) % 4, (z + 3) % 4, (z + 2) % 4
    yp, ym = (y + 1) % 4, (y + 3) % 4
    y2 = (y + 2) % 4
    xo, ho, co = 1 - xl, 1 - xh, 1 - c
    Y_UP, Y_DN, X_HI = tp_dev(xh, yp), tp_dev(xh, ym), tp_dev(ho, y)
    Z_UP, Z_DN = fs_dev(zp, xl, c), fs_dev(zm, xl, c)
    X_LO, CORE = fs_dev(z, xo, c), fs_dev(z, xl, co)

    def remote(src, dst, ss, rs, dev):
        return pltpu.make_async_remote_copy(
            src_ref=src, dst_ref=dst, send_sem=ss, recv_sem=rs, device_id=dev, device_id_type=MESH)

    def rows(a, b, d):
        return (a * 4 + b * 2 + d) * BL

    own = rows(z, xl, c)
    loads = [
        pltpu.make_async_copy(attn_in.at[pl.ds(0, HB)], attn.at[pl.ds(c * HB, HB)], sem_in.at[0]),
        pltpu.make_async_copy(attn_in.at[pl.ds(HB, HB)], attn.at[pl.ds(BL + c * HB, HB)], sem_in.at[1]),
        pltpu.make_async_copy(wout_in, wout, sem_in.at[2]),
        pltpu.make_async_copy(stu_in, stu.at[pl.ds(own, BL)], sem_in.at[3]),
        pltpu.make_async_copy(wal_in, wal, sem_in.at[4]),
    ]
    for l in loads:
        l.start()

    barrier = pltpu.get_barrier_semaphore()
    for i in range(1, 16):
        pl.semaphore_signal(barrier, inc=1, device_id={"tp": t, "fsdp": (f + i) % 16}, device_id_type=MESH)
    for i in range(1, 8):
        pl.semaphore_signal(barrier, inc=1, device_id={"tp": (t + i) % 8, "fsdp": f}, device_id_type=MESH)
    pl.semaphore_wait(barrier, 22)

    def slot(j, d=None):
        return attn.at[pl.ds(j * BL + (c if d is None else d) * HB, HB)]

    def inp(h):
        return attn_in.at[pl.ds(h * HB, HB)]

    def s_rows(blk, d=None, off=0, n=BL):
        return stu.at[pl.ds(rows(blk[0], blk[1], c if d is None else d) + off, n)]

    sends = {}

    def go(name, copy):
        copy().start()
        sends[name] = copy

    def to_core(j):
        go(("core", j), lambda: remote(slot(j), slot(j), sem_cs.at[j], sem_cr.at[j], CORE))

    def from_core(j):
        remote(slot(j, co), slot(j, co), sem_cs.at[j], sem_cr.at[j], CORE).wait_recv()

    def hop(i, src, j, dev):
        go(("hop", i), lambda: remote(src(), slot(j), sem_as.at[i], sem_ar.at[j], dev))

    def landed(j):
        remote(slot(j), slot(j), sem_as.at[0], sem_ar.at[j], X_LO).wait_recv()

    hop(0, lambda: inp(0), 2, Z_UP)
    hop(1, lambda: inp(1), 3, Z_DN)
    hop(2, lambda: inp(0), 4, X_LO)
    hop(3, lambda: inp(1), 7, Z_UP)
    hop(4, lambda: inp(0), 6, Z_DN)
    hop(5, lambda: inp(1), 5, X_LO)
    loads[0].wait()
    loads[1].wait()
    to_core(0)
    to_core(1)

    S_OWN, S_ZM, S_ZP, S_Z2 = (z, xl), (zm, xl), (zp, xl), (z2, xl)
    S_OTHER = [(z, xo), (zm, xo), (zp, xo), (z2, xo)]

    def s_hop(i, src, j, blk, dev, off=0, n=BL):
        go(("stu", i), lambda: remote(src(), s_rows(blk, None, off, n), sem_ss.at[i], sem_sr.at[j], dev))

    def s_landed(j, blk, off=0, n=BL):
        r = s_rows(blk, None, off, n)
        remote(r, r, sem_ss.at[0], sem_sr.at[j], X_LO).wait_recv()

    def s_core(i, blk):
        go(("score", i), lambda: remote(s_rows(blk), s_rows(blk), sem_ss.at[8 + i], sem_sr.at[8 + i], CORE))

    def s_from_core(i, blk):
        r = s_rows(blk, co)
        remote(r, r, sem_ss.at[8 + i], sem_sr.at[8 + i], CORE).wait_recv()

    s_hop(0, lambda: stu_in, 0, S_OWN, Z_UP)
    s_hop(1, lambda: stu_in, 1, S_OWN, Z_DN)
    s_hop(2, lambda: stu_in, 4, S_OWN, X_LO)
    loads[2].wait()
    loads[3].wait()
    s_core(0, S_OWN)
    loads[4].wait()
    acc[...] = jnp.zeros_like(acc)
    lacc[...] = jnp.zeros_like(lacc)

    def event(e):
        if e == 1:
            landed(2)
            hop(6, lambda: slot(2), 8, Z_UP)
            to_core(2)
            landed(3)
            hop(7, lambda: slot(3), 9, Z_DN)
            to_core(3)
            landed(4)
            hop(8, lambda: slot(4), 10, Z_UP)
            to_core(4)
        elif e == 2:
            landed(5)
            hop(10, lambda: slot(5), 11, Z_DN)
            to_core(5)
            landed(6)
            to_core(6)
            landed(7)
            to_core(7)
        elif e == 3:
            s_landed(0, S_ZM)
            s_hop(3, lambda: s_rows(S_ZM, None, 0, HB), 2, S_ZM, Z_UP, 0, HB)
            s_hop(4, lambda: s_rows(S_ZM), 5, S_ZM, X_LO)
            s_core(1, S_ZM)
            s_landed(1, S_ZP)
            s_hop(5, lambda: s_rows(S_ZP, None, HB, HB), 3, S_ZP, Z_DN, HB, HB)
            s_hop(6, lambda: s_rows(S_ZP), 6, S_ZP, X_LO)
            s_core(2, S_ZP)
            hop(9, lambda: slot(4), 12, Z_DN)
            hop(11, lambda: slot(5), 13, Z_UP)
        elif e == 4:
            landed(8)
            to_core(8)
            landed(9)
            to_core(9)
        elif e == 5:
            landed(10)
            hop(12, lambda: slot(10), 14, Z_UP)
            to_core(10)
            landed(11)
            hop(13, lambda: slot(11), 15, Z_DN)
            to_core(11)
        elif e == 6:
            s_landed(2, S_Z2, 0, HB)
            s_landed(3, S_Z2, HB, HB)
            s_hop(7, lambda: s_rows(S_Z2), 7, S_Z2, X_LO)
            s_core(3, S_Z2)
        elif e == 7:
            landed(12)
            to_core(12)
            landed(13)
            to_core(13)
        elif e == 8:
            for j in range(3):
                s_landed(4 + j, S_OTHER[j])
                s_core(4 + j, S_OTHER[j])
        elif e == 9:
            landed(14)
            to_core(14)
            landed(15)
            to_core(15)
        elif e == 10:
            s_landed(7, S_OTHER[3])
            s_core(7, S_OTHER[3])
        elif e == 11:
            for i, blk in enumerate([S_OWN, S_ZM, S_ZP, S_Z2] + S_OTHER):
                s_from_core(i, blk)

    EVENTS = ((0, (1,)), (1, (2,)), (2, (3,)), (3, (4,)), (4, (5,)), (5, (6, 8, 7)), (6, (10, 9)), (7, (11,)))

    def group(ref, slot, g, off, n):
        return ref[slot, pl.ds(g * GR + off, n), :]

    def relay(r, d):
        s = r % NS
        dev = Y_UP if d == 0 else Y_DN
        return remote(rsend.at[s, d], rrecv.at[r, d], sem_rs.at[s, d], sem_rr.at[r, d], dev)

    def near(r, d):
        s = r % NS
        dev = Y_UP if d == 0 else Y_DN
        return remote(nsend.at[s, d], nrecv.at[r, d], sem_ns.at[s, d], sem_nr.at[r, d], dev)

    def across(r):
        s = r % NS
        return remote(xsend.at[s], xrecv.at[r], sem_xs.at[s], sem_xr.at[r], X_HI)

    def stage0_send(r):
        s = r % NS
        rsend[s, 0] = group(part, s, y2, 0, HF).astype(BF)
        relay(r, 0).start()
        rsend[s, 1] = group(part, s, y2, HF, HF).astype(BF)
        relay(r, 1).start()

    def stage0_student(r):
        base = pl.multiple_of((r - NC) * CH, CH)
        at = lax.broadcasted_iota(jnp.int32, (CH, 1), 0)
        row = base + ((at // GR) % 2) * BL + (at // BL) * HB + at % GR
        pick = jnp.where(row == perm_ref[...], 1.0, 0.0).astype(BF)
        mine = jnp.dot(pick, stu[...], preferred_element_type=F32).astype(BF)
        stup[pl.ds(base, CH), :] = mine
        part[r % NS] = jnp.dot(mine, wal[...], preferred_element_type=F32)

    def stage1(r):
        s = r % NS
        relay(r, 0).wait()
        nsend[s, 0, 0:HF, :] = (group(part, s, yp, 0, HF) + rrecv[r, 0].astype(F32)).astype(BF)
        nsend[s, 0, HF:GR, :] = group(part, s, yp, HF, HF).astype(BF)
        near(r, 0).start()
        relay(r, 1).wait()
        nsend[s, 1, 0:HF, :] = group(part, s, ym, 0, HF).astype(BF)
        nsend[s, 1, HF:GR, :] = (group(part, s, ym, HF, HF) + rrecv[r, 1].astype(F32)).astype(BF)
        near(r, 1).start()

    def stage2(r):
        s = r % NS
        near(r, 0).wait()
        near(r, 1).wait()

        def half(h):
            o = pl.multiple_of(h * HF, HF)
            return (group(part, s, y, o, HF) + nrecv[r, 0, pl.ds(o, HF), :].astype(F32)
                    + nrecv[r, 1, pl.ds(o, HF), :].astype(F32))

        xsend[s] = half(ho)
        across(r).start()
        keep[s] = half(xh)

    def stat_copy(k, i):
        return remote(ssend.at[k], srecv.at[k, f], sem_ts.at[k], sem_tr.at[k],
                      {"tp": t, "fsdp": (f + i) % 16})

    def lanes_of(cols):
        lane = lax.broadcasted_iota(jnp.int32, (HF, 128), 1)
        m = jnp.zeros((HF, 128), F32)
        for j, col in enumerate(cols):
            m = jnp.where(lane == j, col, m)
        m = jnp.concatenate([m, jnp.zeros((128 - HF, 128), F32)], axis=0)
        return m.T[0:8, :]

    def stage3(r):
        s = r % NS
        across(r).wait()
        full = keep[s] + xrecv[r]

        @pl.when(r < NC)
        def _():
            side = jnp.logical_or(jnp.logical_or(r == 1, r == 3), jnp.logical_or(r == 5, r == 6))
            low = jnp.logical_or(r == 1, r == 5) == (y < 2)
            dz = jnp.where(side, jnp.where(low, 3, 1), jnp.where(jnp.logical_or(r == 4, r == 7), 2, 0))
            other = jnp.logical_or(r == 2, r >= 5)
            q = ((z + dz) % 4) * 2 + jnp.where(other, xo, xl)
            town[q] = full.astype(BF)

        @pl.when(r >= NC)
        def _():
            k = r - NC
            tg = town[k].astype(F32)
            pown[k] = full
            ssend[k] = lanes_of([jnp.sum(full * tg, axis=1, keepdims=True),
                                 jnp.sum(full * full, axis=1, keepdims=True),
                                 jnp.sum(tg * tg, axis=1, keepdims=True)])
            srecv[k, f] = ssend[k]
            for i in range(1, 16):
                stat_copy(k, i).start()

    def g_rows(k, g, h):
        return gall.at[pl.ds(pl.multiple_of(k * CH + g * GR + h * HF, HF), HF)]

    def g_across(k, h):
        return remote(g_rows(k, y, h), g_rows(k, y, h), sem_xs.at[NS + k], sem_xr.at[2 * NC + k], X_HI)

    def g_near(k, d, h, g):
        return remote(g_rows(k, g, h), g_rows(k, g, h), sem_gs.at[k, d, h], sem_gr.at[k, d, h],
                      Y_UP if d == 0 else Y_DN)

    def g_far(k, d, g):
        return remote(g_rows(k, g, d), g_rows(k, g, d), sem_fs.at[k, d], sem_fr.at[k, d],
                      Y_UP if d == 0 else Y_DN)

    def stage4(k):
        w = remote(srecv.at[k, pl.ds(0, 15)], srecv.at[k, pl.ds(0, 15)], sem_ts.at[k], sem_tr.at[k], CORE)
        w.wait_recv()
        w.wait_send()
        st = srecv[k, 0]
        for i in range(1, 16):
            st = st + srecv[k, i]
        dots, pp, qq = st[0:1, :], st[1:2, :], st[2:3, :]
        n_p, n_t = jnp.sqrt(pp + 1e-6), jnp.sqrt(qq + 1e-6)
        cosine = dots / (n_p * n_t)
        lane = lax.broadcasted_iota(jnp.int32, (1, 128), 1)
        lacc[0:1, :] += jnp.where(lane < HF, 1.0 - cosine, 0.0)
        scale = 16 * 1024 / 32.0
        ca = -scale / (n_p * n_t)
        cb = scale * (cosine / (n_p * n_p))
        both = jnp.concatenate([ca, cb, jnp.zeros((126, 128), F32)], axis=0).T
        g = both[0:HF, 0:1] * town[k].astype(F32) + both[0:HF, 1:2] * pown[k]
        gall[pl.ds(pl.multiple_of(k * CH + y * GR + xh * HF, HF), HF), :] = g.astype(BF)
        g_across(k, xh).start()
        g_near(k, 0, xh, y).start()
        g_near(k, 1, xh, y).start()

        @pl.when(k == NC - 1)
        def _():
            lrecv[t] = lacc[...]
            for i in range(1, 8):
                remote(lacc, lrecv.at[t], sem_ls.at[0], sem_lr.at[0], {"tp": (t + i) % 8, "fsdp": f}).start()

    def stage5(k):
        g_across(k, xh).wait_send()
        g_across(k, ho).wait_recv()
        g_near(k, 0, ho, y).start()
        g_near(k, 1, ho, y).start()

    def stage6(k):
        g_near(k, 0, 0, ym).wait_recv()
        g_far(k, 0, ym).start()
        g_near(k, 1, 1, yp).wait_recv()
        g_far(k, 1, yp).start()

    def stage7(k):
        g_near(k, 0, 1, ym).wait_recv()
        g_near(k, 1, 0, yp).wait_recv()
        g_far(k, 0, y2).wait_recv()
        g_far(k, 1, y2).wait_recv()
        for d in range(2):
            g_far(k, d, y).wait_send()
            for h in range(2):
                g_near(k, d, h, y).wait_send()
        base = pl.multiple_of(k * CH, CH)

        @pl.when(k < NC - 1)
        def _():
            acc[...] += lax.dot_general(
                stup[pl.ds(base, CH), :], gall[pl.ds(base, CH), :], (((0,), (0,)), ((), ())),
                preferred_element_type=F32)

        @pl.when(k == NC - 2)
        def _():
            out_copy(0).start()
            stut[...] = stup[end, :].T
            out_copy(1).start()

    end = pl.ds((NC - 1) * CH, CH)

    def out_copy(i):
        src, dst = ((acc, acc_out), (stut, stu_out), (gall.at[end], g_out))[i]
        return pltpu.make_async_copy(src, dst, sem_in.at[i])

    def tick(i, carry):
        def when(lo, hi, cond_value):
            return pl.when(jnp.logical_and(cond_value >= lo, cond_value <= hi))

        for d, fn in ((D6, stage6), (D5, stage5), (D4, stage4)):
            @when(NC, LAST, i - d)
            def _(d=d, fn=fn):
                fn(i - d - NC)
        for d, fn in ((D3, stage3), (D2, stage2), (D1, stage1)):
            @when(0, LAST, i - d)
            def _(d=d, fn=fn):
                fn(i - d)
        for k in range(NC):
            @pl.when(i == k)
            def _(k=k):
                from_core(2 * k)
                from_core(2 * k + 1)

        @pl.when(i < NC)
        def _():
            base = pl.multiple_of(i * CH, CH)
            part[i % NS] = jnp.dot(attn[pl.ds(base, CH), :], wout[...], preferred_element_type=F32)

        @when(NC, LAST, i)
        def _():
            stage0_student(i)

        @pl.when(i <= LAST)
        def _():
            stage0_send(i)
        for at, events in EVENTS:
            @pl.when(i == at)
            def _(events=events):
                for e in events:
                    event(e)

        @when(NC, LAST, i - D7)
        def _():
            stage7(i - D7 - NC)
        return carry

    lax.fori_loop(0, LAST + D7 + 1, tick, 0)

    out_copy(2).start()
    for copy in sends.values():
        copy().wait_send()
    w = remote(lrecv.at[pl.ds(0, 7)], lrecv.at[pl.ds(0, 7)], sem_ls.at[0], sem_lr.at[0], CORE)
    w.wait_recv()
    w.wait_send()
    total = lrecv[0]
    for i in range(1, 8):
        total = total + lrecv[i]
    loss_ref[0, 0] = jnp.sum(total) / total_rows
    for i in range(3):
        out_copy(i).wait()


def finish(stu_ref, g_ref, acc_ref, out_ref):
    out_ref[...] = acc_ref[...] + jnp.dot(stu_ref[...], g_ref[...], preferred_element_type=F32)


def local(attn_out, w_out, student, w_align, perm):
    rows_all, width = NC * CH, w_out.shape[1]
    dma = pltpu.SemaphoreType.DMA
    loss, acc, stu_end, g_end = pl.pallas_call(
        kernel,
        name="distill",
        out_shape=(jax.ShapeDtypeStruct((1, 1), F32),
                   jax.ShapeDtypeStruct((w_align.shape[0], width), F32),
                   jax.ShapeDtypeStruct((student.shape[1], CH), BF),
                   jax.ShapeDtypeStruct((CH, width), BF)),
        in_specs=[pl.BlockSpec(memory_space=pl.ANY)] * 4 + [pl.BlockSpec(memory_space=pltpu.VMEM)],
        out_specs=(pl.BlockSpec(memory_space=pltpu.SMEM),) + (pl.BlockSpec(memory_space=pl.ANY),) * 3,
        scratch_shapes=[
            pltpu.VMEM((rows_all, attn_out.shape[1]), BF),
            pltpu.VMEM((rows_all, student.shape[1]), BF),
            pltpu.VMEM((rows_all, student.shape[1]), BF),
            pltpu.VMEM(w_out.shape, BF),
            pltpu.VMEM(w_align.shape, BF),
            pltpu.VMEM((NS, CH, width), F32),
            pltpu.VMEM((NS, 2, HF, width), BF),
            pltpu.VMEM((2 * NC, 2, HF, width), BF),
            pltpu.VMEM((NS, 2, GR, width), BF),
            pltpu.VMEM((2 * NC, 2, GR, width), BF),
            pltpu.VMEM((NS, HF, width), F32),
            pltpu.VMEM((2 * NC, HF, width), F32),
            pltpu.VMEM((NS, HF, width), F32),
            pltpu.VMEM((NC, HF, width), BF),
            pltpu.VMEM((NC, HF, width), F32),
            pltpu.VMEM((student.shape[1], CH), BF),
            pltpu.VMEM((NC, 8, 128), F32),
            pltpu.VMEM((NC, 16, 8, 128), F32),
            pltpu.VMEM((rows_all, width), BF),
            pltpu.VMEM((w_align.shape[0], width), F32),
            pltpu.VMEM((8, 128), F32),
            pltpu.VMEM((8, 8, 128), F32),
            dma((5,)),
            dma((14,)), dma((16,)), dma((16,)), dma((16,)), dma((16,)), dma((16,)),
            dma((NS, 2)), dma((2 * NC, 2)),
            dma((NS, 2)), dma((2 * NC, 2)),
            dma((NS + NC,)), dma((3 * NC,)),
            dma((NC,)), dma((NC,)),
            dma((NC, 2, 2)), dma((NC, 2, 2)),
            dma((NC, 2)), dma((NC, 2)),
            dma((1,)), dma((1,)),
        ],
        compiler_params=pltpu.CompilerParams(
            collective_id=0, has_side_effects=True, vmem_limit_bytes=60 * 2**20),
    )(attn_out, student, w_out, w_align, perm.reshape(1, -1))
    tile = 512
    grad = pl.pallas_call(
        finish,
        name="finish",
        grid=(acc.shape[0] // tile,),
        out_shape=jax.ShapeDtypeStruct(acc.shape, F32),
        in_specs=[pl.BlockSpec((tile, CH), lambda i: (i, 0)), pl.BlockSpec((CH, width), lambda i: (0, 0)),
                  pl.BlockSpec((tile, width), lambda i: (i, 0))],
        out_specs=pl.BlockSpec((tile, width), lambda i: (i, 0)),
    )(stu_end, g_end, acc)
    return loss.reshape(()), grad


def solution(mesh):
    placed = (P("fsdp", "tp"), P("tp", "fsdp"), P("fsdp", "tp"), P("tp", "fsdp"), P())
    return jax.shard_map(
        local, mesh=mesh, in_specs=placed, out_specs=(P(), P("tp", "fsdp")), check_vma=False
    )
```

time: 172 us -> 146 us (0.85); the launches traced: 170 us -> 146 us
  Pallas kernels: 163 us -> 144 us
  local copies, waits for them, and re-layouts: 4.79 us -> 0 us
    pallas_call x1, Pallas kernels: 163 us -> 139 us  [local(): pl.pallas_call(kernel, name='distill', out_shape=(jax.ShapeDtypeStruct((1...]
    unnamed x1 -> x0, local copies, waits for them, and re-layouts: 4.79 us -> none
    pallas_call x0 -> x1, Pallas kernels: none -> 4.33 us  [local(): pl.pallas_call(finish, name='finish', grid=(acc.shape[0] // tile,), out_s...]
where the time goes in v2:
time: 146 us
  Pallas kernels  144 us (99%)
  between operations  2.4 us (2%)
    pallas_call x1, Pallas kernels, local(): pl.pallas_call(kernel, name='distill', out_shape=(jax.ShapeDtypeStruct((1...  139 us
    pallas_call x1, Pallas kernels, local(): pl.pallas_call(finish, name='finish', grid=(acc.shape[0] // tile,), out_s...  4.33 us

profile of v2, /device:TPU:1, one launch (start us, length us, event | category | flops | bytes accessed | tf_op | source)
XLA Modules:
  0.0 146.0 jit_solution(17539357413660312436)
XLA Ops:
  0.6 139.2 %distill.1 = (f32[1,1]{1,0:T(1,128)}, f32[1024,1024]{1,0:T(8,128)}, bf16[1024,256]{1,0:T(8,128)(2,1)}, bf16[256,1024]{1,0:T(8,128)(2,1)}) custom-call(bf16[128,2048]{1,0:T(8,128)(2,1)} %attn_in.1, bf16[128,1024]{1,0:T(8,128)(2,1)} %stu_in.1, bf16[2048,1024]{1,0:T(8,128)(2,1)} %wout_in.1, bf16[1024,1024]{1,0:T(8,128)(2,1)} %wal_in.1, s32[1,2048]{1,0:T(1,128)} %bitcast.2), custom_call_target="tpu_custom_call" | custom-call | tf_op jit(solution)/shard_map/distill/pallas_call | solution.py:454
  139.9 4.3 %finish.1 = f32[1024,1024]{1,0:T(8,128)} custom-call(bf16[1024,256]{1,0:T(8,128)(2,1)} %get-tuple-element.7.stu_ref, bf16[256,1024]{1,0:T(8,128)(2,1)} %get-tuple-element.8.g_ref, f32[1024,1024]{1,0:T(8,128)} %get-tuple-element.9.acc_ref), custom_call_target="tpu_custom_call" | custom-call | tf_op jit(solution)/shard_map/finish/pallas_call | solution.py:500

commit v3 on v2

--- a/solution.py
+++ b/solution.py
@@ -103,8 +103,6 @@
     hop(0, lambda: inp(0), 2, Z_UP)
     hop(1, lambda: inp(1), 3, Z_DN)
     hop(2, lambda: inp(0), 4, X_LO)
-    hop(3, lambda: inp(1), 7, Z_UP)
-    hop(4, lambda: inp(0), 6, Z_DN)
     hop(5, lambda: inp(1), 5, X_LO)
     loads[0].wait()
     loads[1].wait()
@@ -130,6 +128,8 @@
 
     s_hop(0, lambda: stu_in, 0, S_OWN, Z_UP)
     s_hop(1, lambda: stu_in, 1, S_OWN, Z_DN)
+    hop(3, lambda: inp(1), 7, Z_UP)
+    hop(4, lambda: inp(0), 6, Z_DN)
     s_hop(2, lambda: stu_in, 4, S_OWN, X_LO)
     loads[2].wait()
     loads[3].wait()
@@ -147,12 +147,15 @@
             hop(7, lambda: slot(3), 9, Z_DN)
             to_core(3)
             landed(4)
-            hop(8, lambda: slot(4), 10, Z_UP)
             to_core(4)
         elif e == 2:
+            hop(8, lambda: slot(4), 10, Z_UP)
             landed(5)
             hop(10, lambda: slot(5), 11, Z_DN)
             to_core(5)
+            hop(9, lambda: slot(4), 12, Z_DN)
+            hop(11, lambda: slot(5), 13, Z_UP)
+        elif e == 12:
             landed(6)
             to_core(6)
             landed(7)
@@ -166,8 +169,6 @@
             s_hop(5, lambda: s_rows(S_ZP, None, HB, HB), 3, S_ZP, Z_DN, HB, HB)
             s_hop(6, lambda: s_rows(S_ZP), 6, S_ZP, X_LO)
             s_core(2, S_ZP)
-            hop(9, lambda: slot(4), 12, Z_DN)
-            hop(11, lambda: slot(5), 13, Z_UP)
         elif e == 4:
             landed(8)
             to_core(8)
@@ -206,7 +207,7 @@
             for i, blk in enumerate([S_OWN, S_ZM, S_ZP, S_Z2] + S_OTHER):
                 s_from_core(i, blk)
 
-    EVENTS = ((0, (1,)), (1, (2,)), (2, (3,)), (3, (4,)), (4, (5,)), (5, (6, 8, 7)), (6, (10, 9)), (7, (11,)))
+    EVENTS = ((0, (1,)), (1, (3, 2)), (2, (12,)), (3, (4,)), (4, (6, 8, 5)), (5, (10, 11)), (6, (7,)), (7, (9,)))
 
     def group(ref, slot, g, off, n):
         return ref[slot, pl.ds(g * GR + off, n), :]
@@ -232,8 +233,19 @@
         rsend[s, 1] = group(part, s, y2, HF, HF).astype(BF)
         relay(r, 1).start()
 
+    T_AT = (0, 1, 2, 3, 4, 5, 7, 9)
+
+    def is_teacher(r):
+        return jnp.logical_or(r < 6, jnp.logical_or(r == 7, r == 9))
+
+    def teacher_chunk(r):
+        return jnp.where(r < 6, r, jnp.where(r == 7, 6, 7))
+
+    def student_chunk(r):
+        return jnp.where(r == 6, 0, jnp.where(r == 8, 1, r - NC))
+
     def stage0_student(r):
-        base = pl.multiple_of((r - NC) * CH, CH)
+        base = pl.multiple_of(student_chunk(r) * CH, CH)
         at = lax.broadcasted_iota(jnp.int32, (CH, 1), 0)
         row = base + ((at // GR) % 2) * BL + (at // BL) * HB + at % GR
         pick = jnp.where(row == perm_ref[...], 1.0, 0.0).astype(BF)
@@ -283,26 +295,28 @@
         across(r).wait()
         full = keep[s] + xrecv[r]
 
-        @pl.when(r < NC)
-        def _():
-            side = jnp.logical_or(jnp.logical_or(r == 1, r == 3), jnp.logical_or(r == 5, r == 6))
-            low = jnp.logical_or(r == 1, r == 5) == (y < 2)
-            dz = jnp.where(side, jnp.where(low, 3, 1), jnp.where(jnp.logical_or(r == 4, r == 7), 2, 0))
-            other = jnp.logical_or(r == 2, r >= 5)
+        @pl.when(is_teacher(r))
+        def _():
+            n = teacher_chunk(r)
+            side = jnp.logical_or(jnp.logical_or(n == 1, n == 3), jnp.logical_or(n == 5, n == 6))
+            low = jnp.logical_or(n == 1, n == 5) == (y < 2)
+            dz = jnp.where(side, jnp.where(low, 3, 1), jnp.where(jnp.logical_or(n == 4, n == 7), 2, 0))
+            other = jnp.logical_or(n == 2, n >= 5)
             q = ((z + dz) % 4) * 2 + jnp.where(other, xo, xl)
             town[q] = full.astype(BF)
 
-        @pl.when(r >= NC)
-        def _():
-            k = r - NC
-            tg = town[k].astype(F32)
-            pown[k] = full
-            ssend[k] = lanes_of([jnp.sum(full * tg, axis=1, keepdims=True),
-                                 jnp.sum(full * full, axis=1, keepdims=True),
-                                 jnp.sum(tg * tg, axis=1, keepdims=True)])
-            srecv[k, f] = ssend[k]
-            for i in range(1, 16):
-                stat_copy(k, i).start()
+        @pl.when(jnp.logical_not(is_teacher(r)))
+        def _():
+            pown[student_chunk(r)] = full
+
+    def stats(k):
+        tg, full = town[k].astype(F32), pown[k]
+        ssend[k] = lanes_of([jnp.sum(full * tg, axis=1, keepdims=True),
+                             jnp.sum(full * full, axis=1, keepdims=True),
+                             jnp.sum(tg * tg, axis=1, keepdims=True)])
+        srecv[k, f] = ssend[k]
+        for i in range(1, 16):
+            stat_copy(k, i).start()
 
     def g_rows(k, g, h):
         return gall.at[pl.ds(pl.multiple_of(k * CH + g * GR + h * HF, HF), HF)]
@@ -399,18 +413,26 @@
             @when(0, LAST, i - d)
             def _(d=d, fn=fn):
                 fn(i - d)
+            if fn is stage3:
+                @pl.when(i == T_AT[-1] + D3)
+                def _():
+                    stats(0)
+
+                @when(1, NC - 1, i - D3 - NC)
+                def _():
+                    stats(i - D3 - NC)
         for k in range(NC):
-            @pl.when(i == k)
+            @pl.when(i == T_AT[k])
             def _(k=k):
                 from_core(2 * k)
                 from_core(2 * k + 1)
 
-        @pl.when(i < NC)
-        def _():
-            base = pl.multiple_of(i * CH, CH)
+        @pl.when(is_teacher(i))
+        def _():
+            base = pl.multiple_of(teacher_chunk(i) * CH, CH)
             part[i % NS] = jnp.dot(attn[pl.ds(base, CH), :], wout[...], preferred_element_type=F32)
 
-        @when(NC, LAST, i)
+        @pl.when(jnp.logical_and(i <= LAST, jnp.logical_not(is_teacher(i))))
         def _():
             stage0_student(i)
 

time: 146 us -> 145 us (level)
  Pallas kernels: 144 us -> 142 us
where the time goes in v3:
time: 145 us
  Pallas kernels  142 us (98%)
  between operations  2.4 us (2%)
    pallas_call x1, Pallas kernels, local(): pl.pallas_call(kernel, name='distill', out_shape=(jax.ShapeDtypeStruct((1...  138 us
    pallas_call x1, Pallas kernels, local(): pl.pallas_call(finish, name='finish', grid=(acc.shape[0] // tile,), out_s...  4.33 us

profile of v3, /device:TPU:1, one launch (start us, length us, event | category | flops | bytes accessed | tf_op | source)
XLA Modules:
  0.0 144.8 jit_solution(11236322237106135567)
XLA Ops:
  0.6 138.1 %distill.1 = (f32[1,1]{1,0:T(1,128)}, f32[1024,1024]{1,0:T(8,128)}, bf16[1024,256]{1,0:T(8,128)(2,1)}, bf16[256,1024]{1,0:T(8,128)(2,1)}) custom-call(bf16[128,2048]{1,0:T(8,128)(2,1)} %attn_in.1, bf16[128,1024]{1,0:T(8,128)(2,1)} %stu_in.1, bf16[2048,1024]{1,0:T(8,128)(2,1)} %wout_in.1, bf16[1024,1024]{1,0:T(8,128)(2,1)} %wal_in.1, s32[1,2048]{1,0:T(1,128)} %bitcast.2), custom_call_target="tpu_custom_call" | custom-call | tf_op jit(solution)/shard_map/distill/pallas_call | solution.py:476
  138.7 4.3 %finish.1 = f32[1024,1024]{1,0:T(8,128)} custom-call(bf16[1024,256]{1,0:T(8,128)(2,1)} %get-tuple-element.7.stu_ref, bf16[256,1024]{1,0:T(8,128)(2,1)} %get-tuple-element.8.g_ref, f32[1024,1024]{1,0:T(8,128)} %get-tuple-element.9.acc_ref), custom_call_target="tpu_custom_call" | custom-call | tf_op jit(solution)/shard_map/finish/pallas_call | solution.py:522

commit v4 on v3

--- a/solution.py
+++ b/solution.py
@@ -134,8 +134,6 @@
     loads[2].wait()
     loads[3].wait()
     s_core(0, S_OWN)
-    loads[4].wait()
-    acc[...] = jnp.zeros_like(acc)
     lacc[...] = jnp.zeros_like(lacc)
 
     def event(e):
@@ -204,6 +202,7 @@
             s_landed(7, S_OTHER[3])
             s_core(7, S_OTHER[3])
         elif e == 11:
+            loads[4].wait()
             for i, blk in enumerate([S_OWN, S_ZM, S_ZP, S_Z2] + S_OTHER):
                 s_from_core(i, blk)
 
@@ -383,11 +382,18 @@
                 g_near(k, d, h, y).wait_send()
         base = pl.multiple_of(k * CH, CH)
 
-        @pl.when(k < NC - 1)
-        def _():
-            acc[...] += lax.dot_general(
+        def product():
+            return lax.dot_general(
                 stup[pl.ds(base, CH), :], gall[pl.ds(base, CH), :], (((0,), (0,)), ((), ())),
                 preferred_element_type=F32)
+
+        @pl.when(k == 0)
+        def _():
+            acc[...] = product()
+
+        @pl.when(jnp.logical_and(k > 0, k < NC - 1))
+        def _():
+            acc[...] += product()
 
         @pl.when(k == NC - 2)
         def _():

time: 145 us -> 145 us (level)
  no operation moved by 1% of the time
where the time goes in v4:
time: 145 us
  Pallas kernels  142 us (98%)
  between operations  2.4 us (2%)
    pallas_call x1, Pallas kernels, local(): pl.pallas_call(kernel, name='distill', out_shape=(jax.ShapeDtypeStruct((1...  138 us
    pallas_call x1, Pallas kernels, local(): pl.pallas_call(finish, name='finish', grid=(acc.shape[0] // tile,), out_s...  4.33 us

profile of v4, /device:TPU:1, one launch (start us, length us, event | category | flops | bytes accessed | tf_op | source)
XLA Modules:
  0.0 144.8 jit_solution(12121390729040447489)
XLA Ops:
  0.6 138.1 %distill.1 = (f32[1,1]{1,0:T(1,128)}, f32[1024,1024]{1,0:T(8,128)}, bf16[1024,256]{1,0:T(8,128)(2,1)}, bf16[256,1024]{1,0:T(8,128)(2,1)}) custom-call(bf16[128,2048]{1,0:T(8,128)(2,1)} %attn_in.1, bf16[128,1024]{1,0:T(8,128)(2,1)} %stu_in.1, bf16[2048,1024]{1,0:T(8,128)(2,1)} %wout_in.1, bf16[1024,1024]{1,0:T(8,128)(2,1)} %wal_in.1, s32[1,2048]{1,0:T(1,128)} %bitcast.2), custom_call_target="tpu_custom_call" | custom-call | tf_op jit(solution)/shard_map/distill/pallas_call | solution.py:482
  138.7 4.3 %finish.1 = f32[1024,1024]{1,0:T(8,128)} custom-call(bf16[1024,256]{1,0:T(8,128)(2,1)} %get-tuple-element.7.stu_ref, bf16[256,1024]{1,0:T(8,128)(2,1)} %get-tuple-element.8.g_ref, f32[1024,1024]{1,0:T(8,128)} %get-tuple-element.9.acc_ref), custom_call_target="tpu_custom_call" | custom-call | tf_op jit(solution)/shard_map/finish/pallas_call | solution.py:528
